TPU v7x, 32 devices: a whole 2x2x4 slice. The times are simulated.
32 devices in a mesh: grp: 2 (over y), tile: 8 (over z, x), mode: 2 (over core).
Axes of the slice: x: 2, y: 2, z: 4, core: 2. Of those that a mesh axis runs over, the one named last changes fastest.
Arguments:
- object_slab: float32 [2048, 2, 256], P(('grp', 'tile')), parts along dimension 0, may hold values from -6 to 6
- probe_modes: float32 [16, 128, 256], P(('grp', 'mode')), parts along dimension 0, may hold values from -1.2 to 1.2
- frames: float32 [64, 128, 128], P(('grp', 'tile')), parts along dimension 0, may hold values from 0.1 to 10
- offsets: int32 [64, 2], P(('grp', 'tile')), parts along dimension 0, may hold values from 0 to 128, as said below
- counts: int32 [16], P(('grp', 'tile')), parts along dimension 0, may hold values from 0 to 4, as said below
Outputs:
- updated_object: float32 [2048, 2, 256], P(('grp', 'tile')), parts along dimension 0
- probe_direction: float32 [16, 128, 256], P(('grp', 'mode')), parts along dimension 0
There are 2 independent parts, one for each index of `grp`. A program takes and returns all parts, laid end to end along the dimension named above; each array names one. Nothing has to cross between parts.
Inputs may be any that keep to these rules, and one draw needn't show every extreme that they name: `offsets`: rows lie in 0 to 127, columns in 0 to 128. For every tile t below 4, counts[t] + counts[t + 4] <= 4; some tile holds 4 live positions.
All inputs are finite; a program needn't handle non-finite values.
Results may differ from a plain program's by a relative error of at most 0.0068.
Values sent between devices are 32-bit elements; how exact they have to be, the bound alone decides.
A program may use at most 64 MiB of HBM per device.

v0:
```python
import jax
import jax.numpy as jnp
from jax import lax
from jax.sharding import PartitionSpec as P

FRAME = 128


def passed_along(x, axis, by):
    count = lax.axis_size(axis)
    pairs = [(i, i + by) for i in range(count) if 0 <= i + by < count]
    return lax.ppermute(x, axis, pairs)


def dft_tables():
    indices = jnp.arange(FRAME, dtype=jnp.int32)
    phases = (indices[:, None] * indices[None, :] % FRAME).astype(jnp.float32) * (
        2.0 * jnp.pi / FRAME
    )
    norm_scale = 1.0 / jnp.sqrt(jnp.float32(FRAME))
    cos_part = (jnp.cos(phases) * norm_scale).astype(jnp.bfloat16)
    sin_part = (-jnp.sin(phases) * norm_scale).astype(jnp.bfloat16)
    right_fwd = jnp.concatenate(
        [jnp.concatenate([cos_part, sin_part], 1), jnp.concatenate([-sin_part, cos_part], 1)], 0
    )
    right_inv = jnp.concatenate(
        [jnp.concatenate([cos_part, -sin_part], 1), jnp.concatenate([sin_part, cos_part], 1)], 0
    )
    return (cos_part, sin_part, right_fwd, right_inv)


def rotate_half(values):
    middle = values.shape[-1] // 2
    return jnp.concatenate([-values[..., middle:], values[..., :middle]], -1)


def complex_product(left, right):
    middle = left.shape[-1] // 2
    lre, lim = (left[..., :middle], left[..., middle:])
    rre, rim = (right[..., :middle], right[..., middle:])
    return jnp.concatenate([lre * rre - lim * rim, lre * rim + lim * rre], -1)


def conjugate_product(left, right):
    middle = left.shape[-1] // 2
    lre, lim = (left[..., :middle], left[..., middle:])
    rre, rim = (right[..., :middle], right[..., middle:])
    return jnp.concatenate([lre * rre + lim * rim, lre * rim - lim * rre], -1)


def transform(values, right_table, cos_part, sin_part, sign):
    first = jnp.einsum(
        "nmrc,cd->nmrd", values, right_table, preferred_element_type=jnp.float32
    ).astype(jnp.bfloat16)
    real_left = jnp.einsum("jr,nmrd->nmjd", cos_part, first, preferred_element_type=jnp.float32)
    imag_left = jnp.einsum("jr,nmrd->nmjd", sin_part, first, preferred_element_type=jnp.float32)
    return real_left + sign * rotate_half(imag_left)


def solve_slots(patch_set, frame_set, probe_modes, tables):
    cos_part, sin_part, right_fwd, right_inv = tables
    frame_size = frame_set.shape[-1]
    psi_waves = complex_product(probe_modes[None], patch_set[:, None]).astype(jnp.bfloat16)
    far_field = transform(psi_waves, right_fwd, cos_part, sin_part, 1.0)
    local_power = jnp.sum(far_field[..., :frame_size] ** 2 + far_field[..., frame_size:] ** 2, 1)
    local_probe = jnp.sum(
        probe_modes[..., :frame_size] ** 2 + probe_modes[..., frame_size:] ** 2, 0
    )
    power, probe_power = lax.psum((local_power, local_probe), "mode")
    factor = jnp.sqrt(frame_set) / jnp.sqrt(power + 1.0) - 1.0
    corrected = (far_field * jnp.concatenate([factor, factor], -1)[:, None]).astype(jnp.bfloat16)
    back_waves = transform(corrected, right_inv, cos_part, sin_part, -1.0)
    gradient = jnp.sum(conjugate_product(probe_modes[None], back_waves), 1)
    probe_part = jnp.sum(conjugate_product(patch_set[:, None], back_waves), 0)
    gradient = lax.psum(gradient, "mode")
    return (gradient, probe_part, probe_power)


def body(object_slab, probe_modes, frames, offsets, counts):
    tables = dft_tables()
    tile_rows = object_slab.shape[0]
    columns = object_slab.shape[2]
    frame_size = frames.shape[1]
    slots = frames.shape[0]
    zero_index = jnp.int32(0)
    below = passed_along(object_slab, "tile", -1)
    extended = jnp.concatenate([object_slab, below], 0)
    live_count = counts[0]
    slot_ids = jnp.arange(slots, dtype=jnp.int32)
    live_mask = slot_ids < live_count
    row_start = offsets[:, 0]
    col_start = offsets[:, 1]

    def cut_patch(row_at, col_at):
        return lax.dynamic_slice(
            extended, (row_at, zero_index, col_at), (frame_size, 2, frame_size)
        )

    patches = jax.vmap(cut_patch)(row_start, col_start).reshape(slots, frame_size, 2 * frame_size)
    patches = patches * live_mask[:, None, None].astype(jnp.float32)
    grad_patches, probe_part, probe_power = solve_slots(patches, frames, probe_modes, tables)
    grad_patches = grad_patches.reshape(slots, frame_size, 2, frame_size)

    def add_patch(slot_id, slabs):
        grad_now, illum_now = slabs
        row_at = row_start[slot_id]
        col_at = col_start[slot_id]
        old_grad = lax.dynamic_slice(
            grad_now, (row_at, zero_index, col_at), (frame_size, 2, frame_size)
        )
        grad_now = lax.dynamic_update_slice(
            grad_now, old_grad + grad_patches[slot_id], (row_at, zero_index, col_at)
        )
        old_illum = lax.dynamic_slice(illum_now, (row_at, col_at), (frame_size, frame_size))
        weight = live_mask[slot_id].astype(jnp.float32)
        illum_now = lax.dynamic_update_slice(
            illum_now, old_illum + probe_power * weight, (row_at, col_at)
        )
        return (grad_now, illum_now)

    empty_grad = jnp.zeros((2 * tile_rows, 2, columns), jnp.float32)
    empty_illum = jnp.zeros((2 * tile_rows, columns), jnp.float32)
    grad_ext, illum_ext = lax.fori_loop(0, slots, add_patch, (empty_grad, empty_illum))
    spill_grad, spill_illum = passed_along((grad_ext[tile_rows:], illum_ext[tile_rows:]), "tile", 1)
    gradient = grad_ext[:tile_rows] + spill_grad
    illumination = illum_ext[:tile_rows] + spill_illum
    peak = lax.pmax(jnp.max(illumination), "tile")
    updated_object = object_slab + gradient / (illumination[:, None, :] + 0.1 * peak)
    probe_total = lax.psum(probe_part, "tile")
    probe_direction = probe_total / jnp.sqrt(jnp.float32(lax.axis_size("tile") * slots))
    return (updated_object, probe_direction)


def solution(mesh):
    placed = (
        P(("grp", "tile"), None, None),
        P(("grp", "mode"), None, None),
        P(("grp", "tile"), None, None),
        P(("grp", "tile"), None),
        P(("grp", "tile")),
    )
    return jax.shard_map(
        body,
        mesh=mesh,
        in_specs=placed,
        out_specs=(P(("grp", "tile"), None, None), P(("grp", "mode"), None, None)),
        check_vma=False,
    )
```

profile of v0, /device:TPU:0, one launch (start us, length us, event | category | flops | bytes accessed | tf_op | source)
XLA Modules:
  0.0 245.6 jit_solution(17478681382126986310)
XLA Ops:
  7.2 1.3 collective-permute-start
  10.8 1.1 slice_bitcast_fusion.3
  11.8 6.7 %collective-permute-done = f32[128,2,256]{2,1,0:T(2,128)S(1)} collective-permute-done((f32[128,2,256]{2,1,0:T(2,128)}, f32[128,2,256]{2,1,0:T(2,128)S(1)}, u32[]{:S(2)}, u32[]{:S(2)}) %collective-permute-start) | collective-permute-done | bytes 262176 | tf_op jit(solution)/shard_map/ppermute | solution.py:12
  18.6 1.2 pad_maximum_fusion
  19.7 8.3 %while.17 = (s32[]{:T(128)}, f32[256,2,256]{2,1,0:T(2,128)S(1)}, s32[4,3]{1,0:T(4,128)S(1)}, f32[4,128,2,128]{3,2,1,0:T(2,128)S(1)}, s32[]{:T(128)}) while((s32[]{:T(128)}, f32[256,2,256]{2,1,0:T(2,128)S(1)}, s32[4,3]{1,0:T(4,128)S(1)}, f32[4,128,2,128]{3,2,1,0:T(2,128)S(1)}, s32[]{:T(128)}) %tuple.60), condition=%wide.while_cond, body=%wide.while_body.sunk | while | flops 2 | bytes 262261 | solution.py:95
  20.4 1.5 bitcast_dynamic-update-slice_fusion.2
  22.4 1.5 bitcast_dynamic-update-slice_fusion.2
  24.5 1.5 bitcast_dynamic-update-slice_fusion.2
  26.6 1.5 bitcast_dynamic-update-slice_fusion.2
  32.0 1.1 copy.31
  33.1 1.7 add_reduce_fusion
  34.8 17.0 %all-reduce.5.cloned.1.call-done = f32[4,128,128]{1,2,0:T(8,128)} async-done(((f32[4,128,128]{1,2,0:T(8,128)}), f32[4,128,128]{1,2,0:T(8,128)}) %all-reduce.5.cloned.1.call-update) | async-done | bytes 262160 | tf_op jit(solution)/shard_map/psum | solution.py:69
  51.7 1.0 multiply_add_fusion.3
  55.5 1.1 reshape.32
  57.6 19.2 %all-reduce.9.cloned.1.call-done = (f32[4,128,2,128]{3,2,1,0:T(2,128)}, f32[128,128]{1,0:T(8,128)}) async-done(((f32[4,128,2,128]{3,2,1,0:T(2,128)}, f32[128,128]{1,0:T(8,128)}), (f32[4,128,2,128]{3,2,1,0:T(2,128)}, f32[128,128]{1,0:T(8,128)})) %all-reduce.9.cloned.1.call-update) | async-done | bytes 589840 | tf_op jit(solution)/shard_map/psum | solution.py:75
  76.9 91.1 %while.16 = (s32[]{:T(128)}, f32[256,2,256]{2,1,0:T(2,128)S(1)}, f32[256,256]{1,0:T(8,128)S(1)}, s32[4]{0:T(128)S(1)}, s32[4]{0:T(128)S(1)}, /*index=5*/f32[4,12...) while((s32[]{:T(128)}, f32[256,2,256]{2,1,0:T(2,128)S(1)}, ...), condition=%wide.region_7.8_spmd, body=%wide.region_6.7_spmd.sunk | while | flops 65545 | bytes 983284 | solution.py:123
  82.0 1.1 bitcast_add_fusion.2
  83.1 4.4 %dynamic_update_slice.16 = f32[256,2,256]{2,1,0:T(2,128)S(1)} dynamic-update-slice(f32[256,2,256]{2,1,0:T(2,128)S(1)} %get-tuple-element.309, f32[128,2,128]{2,1,0:T(2,128)S(1)} %bitcast_add_fusion.2, s32[]{:T(128)S(6)} %select_n.95, s32[]{:T(128)} %constant.56.clone.1..sunk, s32[]{:T(128)S(6)} %select_n.96) | dynamic-update-slice | bytes 262148 | tf_op jit(solution)/shard_map/while/body/eval_jaxpr/dynamic_update_slice | solution.py:111
  89.7 1.3 dynamic_update_slice.17
  96.1 1.1 bitcast_add_fusion.2
  97.2 4.2 %dynamic_update_slice.16 = f32[256,2,256]{2,1,0:T(2,128)S(1)} dynamic-update-slice(f32[256,2,256]{2,1,0:T(2,128)S(1)} %get-tuple-element.309, f32[128,2,128]{2,1,0:T(2,128)S(1)} %bitcast_add_fusion.2, s32[]{:T(128)S(6)} %select_n.95, s32[]{:T(128)} %constant.56.clone.1..sunk, s32[]{:T(128)S(6)} %select_n.96) | dynamic-update-slice | bytes 262148 | tf_op jit(solution)/shard_map/while/body/eval_jaxpr/dynamic_update_slice | solution.py:111
  103.6 1.1 dynamic_update_slice.17
  109.8 1.1 bitcast_add_fusion.2
  110.9 21.6 %dynamic_update_slice.16 = f32[256,2,256]{2,1,0:T(2,128)S(1)} dynamic-update-slice(f32[256,2,256]{2,1,0:T(2,128)S(1)} %get-tuple-element.309, f32[128,2,128]{2,1,0:T(2,128)S(1)} %bitcast_add_fusion.2, s32[]{:T(128)S(6)} %select_n.95, s32[]{:T(128)} %constant.56.clone.1..sunk, s32[]{:T(128)S(6)} %select_n.96) | dynamic-update-slice | bytes 262148 | tf_op jit(solution)/shard_map/while/body/eval_jaxpr/dynamic_update_slice | solution.py:111
  134.7 1.7 dynamic_update_slice.17
  141.5 1.1 bitcast_add_fusion.2
  142.6 21.6 %dynamic_update_slice.16 = f32[256,2,256]{2,1,0:T(2,128)S(1)} dynamic-update-slice(f32[256,2,256]{2,1,0:T(2,128)S(1)} %get-tuple-element.309, f32[128,2,128]{2,1,0:T(2,128)S(1)} %bitcast_add_fusion.2, s32[]{:T(128)S(6)} %select_n.95, s32[]{:T(128)} %constant.56.clone.1..sunk, s32[]{:T(128)S(6)} %select_n.96) | dynamic-update-slice | bytes 262148 | tf_op jit(solution)/shard_map/while/body/eval_jaxpr/dynamic_update_slice | solution.py:111
  166.4 1.7 dynamic_update_slice.17
  168.1 39.8 %collective-permute-start.2 = (f32[128,256]{1,0:T(8,128)S(1)}, f32[128,256]{1,0:T(8,128)S(1)}, u32[]{:S(2)}, u32[]{:S(2)}) collective-permute-start(f32[128,256]{1,0:T(8,128)S(1)} %slice.85), channel_id=1, source_target_pairs={{0,2},{2,4},{4,6},{6,8},{8,10},{10,12},{12,14},{1,3},{3,5},{5,7},{... | collective-permute-start | bytes 393224 | tf_op jit(solution)/shard_map/ppermute | solution.py:12
  207.9 3.4 %collective-permute-start.1 = (f32[128,2,256]{2,1,0:T(2,128)S(1)}, f32[128,2,256]{2,1,0:T(2,128)S(1)}, u32[]{:S(2)}, u32[]{:S(2)}) collective-permute-start(f32[128,2,256]{2,1,0:T(2,128)S(1)} %slice.83), channel_id=1, source_target_pairs={{0,2},{2,4},{4,6},{6,8},{8,10},{10,12},{12,14},{1,3},{3,5},{5,7},{... | collective-permute-start | bytes 786440 | tf_op jit(solution)/shard_map/ppermute | solution.py:12
  212.0 1.9 broadcast_multiply_fusion
  213.9 23.5 %pmax.7 = f32[]{:T(128)} all-reduce(f32[]{:T(128)} %fusion.23), channel_id=1, replica_groups=mesh['grp'=2,'tile'=8,'mode'=2] {'tile'}, use_global_device_ids=true, to_apply=%region_9.10 | all-reduce | flops 1 | bytes 8 | tf_op jit(solution)/shard_map/pmax | solution.py:127
  (70 shorter events, 24.1 us)
Async XLA Ops:
  7.2 44.6 %all-reduce.5.cloned.1.call-start = ((), (), s32[]{:S(2)}) async-start(), calls=%async_computation | async-start | bytes 524288 | tf_op jit(solution)/shard_map/psum | solution.py:69
  7.2 11.4 %collective-permute-start = (f32[128,2,256]{2,1,0:T(2,128)}, f32[128,2,256]{2,1,0:T(2,128)S(1)}, u32[]{:S(2)}, u32[]{:S(2)}) collective-permute-start(f32[128,2,256]{2,1,0:T(2,128)} %param.7), channel_id=1, source_target_pairs={{2,0},{4,2},{6,4},{8,6},{10,8},{12,10},{14,12},{3,1},{5,3},{7,5},{... | collective-permute-start | bytes 786440 | tf_op jit(solution)/shard_map/ppermute | solution.py:12
  31.9 44.8 %all-reduce.9.cloned.1.call-start = ((), (), s32[]{:S(2)}) async-start(), calls=%async_computation.2 | async-start | bytes 1179648 | tf_op jit(solution)/shard_map/psum | solution.py:75
  56.6 155.5 %all-reduce.7.cloned.1.call-start = ((), (), s32[]{:S(2)}) async-start(), calls=%async_computation.1 | async-start | bytes 1048576 | tf_op jit(solution)/shard_map/psum | solution.py:129
  168.1 70.0 %copy-start = (f32[128,2,256]{2,1,0:T(2,128)S(1)}, f32[128,2,256]{2,1,0:T(2,128)}, u32[]{:S(2)}) copy-start(f32[128,2,256]{2,1,0:T(2,128)} %param.7) | copy-start | bytes 786436
  168.1 43.3 %collective-permute-start.2 = (f32[128,256]{1,0:T(8,128)S(1)}, f32[128,256]{1,0:T(8,128)S(1)}, u32[]{:S(2)}, u32[]{:S(2)}) collective-permute-start(f32[128,256]{1,0:T(8,128)S(1)} %slice.85), channel_id=1, source_target_pairs={{0,2},{2,4},{4,6},{6,8},{8,10},{10,12},{12,14},{1,3},{3,5},{5,7},{... | collective-permute-start | bytes 393224 | tf_op jit(solution)/shard_map/ppermute | solution.py:12
  207.9 30.2 %collective-permute-start.1 = (f32[128,2,256]{2,1,0:T(2,128)S(1)}, f32[128,2,256]{2,1,0:T(2,128)S(1)}, u32[]{:S(2)}, u32[]{:S(2)}) collective-permute-start(f32[128,2,256]{2,1,0:T(2,128)S(1)} %slice.83), channel_id=1, source_target_pairs={{0,2},{2,4},{4,6},{6,8},{8,10},{10,12},{12,14},{1,3},{3,5},{5,7},{... | collective-permute-start | bytes 786440 | tf_op jit(solution)/shard_map/ppermute | solution.py:12
Sparse Core Ops, SparseCore 0:
  32.1 19.6 all-reduce.4
  56.7 20.0 all-reduce.8
  80.2 74.2 all-reduce.6
where the time goes:
time: 247 us; the launch traced here: 246 us
  local copies, waits for them, and re-layouts  77.6 us (31%)
  starting transfers between devices  44.6 us (18%)
  waiting for transfers between devices  43 us (17%)
  blocking collectives  23.5 us (10%)
  other arithmetic  19.5 us (8%)
  loops' own time  18.4 us (7%)
  between operations  15.3 us (6%)
  matrix products  3.62 us (1%)
    dynamic_update_slice x4, local copies, waits for them, and re-layouts, add_patch(): lax.dynamic_update_slice(grad_now, old_grad + grad_patches[slot_id], (row...  51.7 us
    ppermute x3, starting transfers between devices, passed_along(): return lax.ppermute(x, axis, pairs)  44.5 us
    pmax x1, blocking collectives, body(): peak = lax.pmax(jnp.max(illumination), 'tile')  23.5 us
    psum x1, waiting for transfers between devices, solve_slots(): gradient = lax.psum(gradient, 'mode')  19.2 us
    another operation x1, loops' own time, body(): lax.fori_loop(0, slots, add_patch, (empty_grad, empty_illum))  18.3 us
    psum x1, waiting for transfers between devices, solve_slots(): power, probe_power = lax.psum((local_power, local_probe), 'mode')  17 us
    gather x12, local copies, waits for them, and re-layouts  8.22 us
    ppermute x3, waiting for transfers between devices, passed_along(): return lax.ppermute(x, axis, pairs)  6.73 us
  transfers between devices with their start and end apart: 6, of which 3 were waited for; matrix products, arithmetic and copies ran while one was open for 33% of the time, Pallas kernels for 0%

commit v1 on v0

v1 whole, which is shorter than its diff:
```python
import functools

import jax
import jax.numpy as jnp
import numpy as np
from jax import lax
from jax.experimental import pallas as pl
from jax.experimental.pallas import tpu as pltpu
from jax.sharding import PartitionSpec as P

FRAME = 128
MIN_ROWS = 8


def dft_matrices():
    indices = np.arange(FRAME)
    phases = (indices[:, None] * indices[None, :] % FRAME) * (2.0 * np.pi / FRAME)
    cos_part = np.cos(phases) / np.sqrt(FRAME)
    sin_part = -np.sin(phases) / np.sqrt(FRAME)
    fwd = np.block([[cos_part, sin_part], [-sin_part, cos_part]])
    inv = np.block([[cos_part, -sin_part], [sin_part, cos_part]])
    return fwd.astype(jnp.bfloat16), inv.astype(jnp.bfloat16)


def stages_of(tiles):
    bits = tiles.bit_length() - 1
    assert tiles == 1 << bits
    stages, at, rows = [], 0, FRAME
    while at < bits:
        radix = 2 if at == 0 or bits - at == 1 else 4
        after = rows // radix if rows // radix >= MIN_ROWS else rows
        stages.append((at, radix, rows, after))
        rows = after
        at += 1 if radix == 2 else 2
    return stages


def tree(values, join):
    while len(values) > 1:
        values = [join(values[i], values[i + 1]) for i in range(0, len(values), 2)]
    return values[0]


def kernel(
    tiles,
    stages,
    obj,
    probe,
    frames,
    offsets,
    counts,
    fwd,
    inv,
    obj_out,
    probe_out,
    ext,
    power_probe,
    ext_split,
    illum,
    illum_in,
    patches,
    far,
    power,
    power_in,
    factor,
    grad,
    grad_in,
    gext,
    spill_in,
    acc,
    peaks,
    halo_sem,
    relay_sem,
    pp_sem,
    illum_sem,
    power_sem,
    grad_sem,
    spill_sem,
    upd_sem,
    *staged,
):
    n_st = len(stages)
    rs_in, pk_in = staged[:n_st], staged[n_st : 2 * n_st]
    rs_sem, ag_sem, pk_sem = (staged[(2 + j) * n_st : (3 + j) * n_st] for j in range(3))
    slots = frames.shape[0]
    modes = probe.shape[0]
    f = FRAME
    me = lax.axis_index("tile")
    core = lax.axis_index("mode")
    other = 1 - core
    has_left, has_right = me > 0, me < tiles - 1
    left, right = jnp.maximum(me - 1, 0), jnp.minimum(me + 1, tiles - 1)

    def remote(src, dst, sems, **where):
        return pltpu.make_async_remote_copy(
            src_ref=src,
            dst_ref=dst,
            send_sem=sems[0],
            recv_sem=sems[1],
            device_id=where,
            device_id_type=pl.DeviceIdType.MESH,
        )

    def pair(sem, *at):
        return (sem.at[(0, *at)], sem.at[(1, *at)])

    own_power = jnp.zeros((f, f), jnp.float32)
    for k in range(modes):
        own_power += probe[k, :, :f] ** 2 + probe[k, :, f:] ** 2
    power_probe[0] = own_power

    barrier = pltpu.get_barrier_semaphore()

    def greet(**where):
        pl.semaphore_signal(
            barrier, inc=1, device_id=where, device_id_type=pl.DeviceIdType.MESH
        )

    greet(mode=other)
    greeted = 1
    for at, radix, _, _ in stages:
        for d in range(1, radix):
            greet(tile=me ^ (d << at))
            greeted += 1

    @pl.when(has_left)
    def _():
        greet(tile=left)

    @pl.when(has_right)
    def _():
        greet(tile=right)

    beside = jnp.minimum(me, 1) + jnp.minimum(tiles - 1 - me, 1)
    pl.semaphore_wait(barrier, greeted + beside)

    halo = remote(obj.at[core], ext.at[core, pl.ds(f, f)], pair(halo_sem), tile=left)

    @pl.when(has_left)
    def _():
        halo.start()

    pp_copy = remote(power_probe.at[0], power_probe.at[1], pair(pp_sem), mode=other)
    pp_copy.start()
    ext[:, :f, :] = obj[...]

    def live(s):
        return jnp.clip(counts[0] - s, 0, 1).astype(jnp.float32)

    def dot(a, b):
        return jnp.dot(a, b, preferred_element_type=jnp.float32)

    def split(x):
        high = x.astype(jnp.bfloat16)
        return high, (x - high.astype(jnp.float32)).astype(jnp.bfloat16)

    def shifts(rows, columns, by):
        i = lax.broadcasted_iota(jnp.int32, (rows, columns), 0)
        j = lax.broadcasted_iota(jnp.int32, (rows, columns), 1)
        apart = j - i if rows < columns else i - j
        return jnp.where(apart == by, 1.0, 0.0).astype(jnp.float32)

    def spread(s, values):
        across = shifts(f, 2 * f, offsets[s, 1]).astype(jnp.bfloat16)
        down = (shifts(2 * f, f, offsets[s, 0]) * live(s)).astype(jnp.bfloat16)
        wide = dot(jnp.concatenate(split(values), 0), across).astype(jnp.bfloat16)
        return dot(jnp.concatenate([down, down], 1), wide)

    pp_copy.wait()
    probe_power = power_probe[0] + power_probe[1]
    illum[...] = jnp.zeros_like(illum)

    def light(s, carry):
        illum[...] += spread(s, probe_power)
        return carry

    lax.fori_loop(0, slots, light, 0)
    illum_copy = remote(illum.at[pl.ds(f, f)], illum_in, pair(illum_sem), tile=right)

    @pl.when(has_right)
    def _():
        illum_copy.start()

    relay = remote(
        ext.at[core, pl.ds(f, f)], ext.at[core, pl.ds(f, f)], pair(relay_sem), mode=other
    )

    @pl.when(has_right)
    def _():
        halo.wait_recv()
        relay.start()
        relay.wait_recv()

    @pl.when(jnp.logical_not(has_right))
    def _():
        ext[:, f:, :] = jnp.zeros((2, f, 2 * f), jnp.float32)

    for part in range(2):
        for j, piece in enumerate(split(ext[part])):
            ext_split[:, (2 * part + j) * 2 * f : (2 * part + j + 1) * 2 * f] = piece

    def window(s):
        down = (shifts(f, 2 * f, offsets[s, 0]) * live(s)).astype(jnp.bfloat16)
        across = shifts(2 * f, f, offsets[s, 1]).astype(jnp.bfloat16)
        rows = dot(down, ext_split[...]).astype(jnp.bfloat16)
        both = jnp.concatenate([rows[:, : 4 * f], rows[:, 4 * f :]], 0)
        return dot(both, jnp.concatenate([across, across], 0))

    def swap(x):
        return jnp.concatenate(
            [
                jnp.concatenate([x[:f, :f], x[f:, :f]], 1),
                jnp.concatenate([x[:f, f:], x[f:, f:]], 1),
            ],
            0,
        )

    def power_copy(s):
        return remote(power.at[s], power_in.at[s], pair(power_sem, s), mode=other)

    def forward(s, carry):
        patch = window(s)
        xr, xi = patch[:f], patch[f:]
        patches[s, :, :f] = xr
        patches[s, :, f:] = xi
        total = jnp.zeros((f, f), jnp.float32)
        for p in range(modes // 2):
            psi = []
            for k in (2 * p, 2 * p + 1):
                pr, pi = probe[k, :, :f], probe[k, :, f:]
                psi.append(
                    jnp.concatenate([pr * xr - pi * xi, pr * xi + pi * xr], 1).astype(jnp.bfloat16)
                )
            half = dot(jnp.concatenate(psi, 0), fwd[...]).astype(jnp.bfloat16)
            wave = dot(inv[...], swap(half))
            far[s, p] = wave
            squares = wave * wave
            total += (squares[:f, :f] + squares[f:, :f]) + (squares[:f, f:] + squares[f:, f:])
        power[s] = total
        power_copy(s).start()
        return carry

    lax.fori_loop(0, slots, forward, 0)

    @pl.when(has_left)
    def _():
        illum_copy.wait_recv()

    @pl.when(jnp.logical_not(has_left))
    def _():
        illum_in[...] = jnp.zeros_like(illum_in)

    @pl.when(has_right)
    def _():
        illum_copy.wait_send()

    illum[:f] = illum[:f] + illum_in[...]
    high = jnp.max(illum[:f].reshape(f // 8, 8, 2 * f), 0)
    peaks[0] = jnp.maximum(high[:, :f], high[:, f:])

    def peak_copies(i):
        at, radix, _, _ = stages[i]
        return [
            remote(
                peaks.at[i], pk_in[i].at[d - 1], pair(pk_sem[i], d - 1), tile=me ^ (d << at)
            )
            for d in range(1, radix)
        ]

    def peak_start(i):
        for copy in peak_copies(i):
            copy.start()

    def peak_finish(i):
        for copy in peak_copies(i):
            copy.wait()
        radix = stages[i][1]
        peaks[i + 1] = tree([peaks[i]] + [pk_in[i][d] for d in range(radix - 1)], jnp.maximum)

    peak_start(0)

    def rescale(s, carry):
        power_copy(s).wait()
        factor[s] = (
            jnp.sqrt(frames[s]) * lax.rsqrt(power[s] + power_in[s] + 1.0) - 1.0
        )
        return carry

    lax.fori_loop(0, slots, rescale, 0)

    starts = [0]
    for at, radix, rows, after in stages:
        digit = lax.rem(me // (1 << at), radix)
        starts.append(starts[-1] + digit * after if after < rows else starts[-1])

    def rows_at(ref, k, start, rows):
        return ref.at[k, pl.ds(pl.multiple_of(start, MIN_ROWS), rows)]

    def rs_copies(i, k):
        at, radix, rows, after = stages[i]
        digit = lax.rem(me // (1 << at), radix)
        copies = []
        for d in range(1, radix):
            start = starts[i] + (digit ^ d) * after if after < rows else starts[i]
            copies.append(
                remote(
                    rows_at(acc, k, start, after),
                    rs_in[i].at[k, d - 1],
                    pair(rs_sem[i], k, d - 1),
                    tile=me ^ (d << at),
                )
            )
        return copies

    def rs_start(i, ks):
        for k in ks:
            for copy in rs_copies(i, k):
                copy.start()

    def rs_finish(i, ks):
        after, radix = stages[i][3], stages[i][1]
        for k in ks:
            for copy in rs_copies(i, k):
                copy.wait()
            here = rows_at(acc, k, starts[i + 1], after)
            here[...] = tree(
                [here[...]] + [rs_in[i][k, d] for d in range(radix - 1)], lax.add
            )

    scale = 1.0 / np.sqrt(np.float32(tiles * slots))

    def finish_sum(ks):
        for k in ks:
            last = stages[-1][3]
            rows_at(probe_out, k, starts[-1], last)[...] = (
                rows_at(acc, k, starts[-1], last)[...] * scale
            )

    def ag_copies(i, k):
        at, radix, rows, after = stages[i]
        if after == rows:
            return []
        here = rows_at(probe_out, k, starts[i + 1], after)
        return [
            remote(here, here, pair(ag_sem[i], k, d - 1), tile=me ^ (d << at))
            for d in range(1, radix)
        ]

    def ag_start(i, ks):
        for k in ks:
            for copy in ag_copies(i, k):
                copy.start()

    def ag_finish(i, ks):
        for k in ks:
            for copy in ag_copies(i, k):
                copy.wait()

    groups = [(2 * p, 2 * p + 1) for p in range(modes // 2)]
    for p, ks in enumerate(groups):
        for k in ks:
            acc[k] = jnp.zeros((f, 2 * f), jnp.float32)

        def backward(s, carry, p=p, ks=ks):
            scaled = factor[s]
            wide = jnp.concatenate([scaled, scaled], 1)
            wide = jnp.concatenate([wide, wide], 0)
            corrected = (far[s, p] * wide).astype(jnp.bfloat16)
            half = dot(swap(corrected), inv[...]).astype(jnp.bfloat16)
            back = dot(fwd[...], swap(half))
            xr, xi = patches[s, :, :f], patches[s, :, f:]
            gr, gi = None, None
            for j, k in enumerate(ks):
                br, bi = back[:f, j * f : (j + 1) * f], back[f:, j * f : (j + 1) * f]
                pr, pi = probe[k, :, :f], probe[k, :, f:]
                r, i = pr * br + pi * bi, pr * bi - pi * br
                gr, gi = (r, i) if gr is None else (gr + r, gi + i)
                acc[k, :, :f] += xr * br + xi * bi
                acc[k, :, f:] += xr * bi - xi * br
            if p == 0:
                grad[0, s], grad[1, s] = gr, gi
            else:
                grad[0, s] += gr
                grad[1, s] += gi
            return carry

        lax.fori_loop(0, slots, backward, 0)
        if p == len(groups) - 1:
            grad_copy = remote(grad.at[other], grad_in, pair(grad_sem), mode=other)
            grad_copy.start()
        rs_start(0, ks)
        if p < n_st:
            peak_finish(p)
            if p + 1 < n_st:
                peak_start(p + 1)

    for i in range(len(groups), n_st):
        peak_finish(i)
        if i + 1 < n_st:
            peak_start(i + 1)

    grad_copy.wait()
    gext[...] = jnp.zeros_like(gext)

    def gather_up(s, carry):
        gext[...] += spread(s, grad[core, s] + grad_in[s])
        return carry

    lax.fori_loop(0, slots, gather_up, 0)
    spill_copy = remote(gext.at[pl.ds(f, f)], spill_in, pair(spill_sem), tile=right)

    @pl.when(has_right)
    def _():
        spill_copy.start()

    for i in range(n_st):
        for ks in groups:
            rs_finish(i, ks)
            if i + 1 < n_st:
                rs_start(i + 1, ks)
            else:
                finish_sum(ks)
                ag_start(i, ks)

    @pl.when(has_left)
    def _():
        spill_copy.wait_recv()

    @pl.when(jnp.logical_not(has_left))
    def _():
        spill_in[...] = jnp.zeros_like(spill_in)

    peak = jnp.max(peaks[n_st])
    obj_out[core] = obj[core] + (gext[:f] + spill_in[...]) / (illum[:f] + 0.1 * peak)
    upd_copy = remote(obj_out.at[core], obj_out.at[core], pair(upd_sem), mode=other)
    upd_copy.start()

    for i in reversed(range(n_st)):
        for ks in groups:
            ag_finish(i, ks)
            if i > 0:
                ag_start(i - 1, ks)

    upd_copy.wait()

    @pl.when(has_left)
    def _():
        halo.wait_send()

    @pl.when(has_right)
    def _():
        relay.wait_send()
        spill_copy.wait_send()


def body(tiles, object_slab, probe_modes, frames, offsets, counts):
    f = FRAME
    stages = stages_of(tiles)
    slots, modes = frames.shape[0], probe_modes.shape[0]
    columns = object_slab.shape[2]
    fwd, inv = dft_matrices()
    f32 = jnp.float32
    vmem = pl.BlockSpec(memory_space=pltpu.VMEM)
    smem = pl.BlockSpec(memory_space=pltpu.SMEM)
    dma = pltpu.SemaphoreType.DMA
    scratch = [
        pltpu.VMEM((2, 2 * f, columns), f32),
        pltpu.VMEM((2, f, f), f32),
        pltpu.VMEM((2 * f, 4 * columns), jnp.bfloat16),
        pltpu.VMEM((2 * f, columns), f32),
        pltpu.VMEM((f, columns), f32),
        pltpu.VMEM((slots, f, 2 * f), f32),
        pltpu.VMEM((slots, modes // 2, 2 * f, 2 * f), f32),
        pltpu.VMEM((slots, f, f), f32),
        pltpu.VMEM((slots, f, f), f32),
        pltpu.VMEM((slots, f, f), f32),
        pltpu.VMEM((2, slots, f, f), f32),
        pltpu.VMEM((slots, f, f), f32),
        pltpu.VMEM((2 * f, columns), f32),
        pltpu.VMEM((f, columns), f32),
        pltpu.VMEM((modes, f, 2 * f), f32),
        pltpu.VMEM((len(stages) + 1, 8, f), f32),
        dma((2,)),
        dma((2,)),
        dma((2,)),
        dma((2,)),
        dma((2, slots)),
        dma((2,)),
        dma((2,)),
        dma((2,)),
    ]
    scratch += [pltpu.VMEM((modes, radix - 1, after, 2 * f), f32) for _, radix, _, after in stages]
    scratch += [pltpu.VMEM((radix - 1, 8, f), f32) for _, radix, _, _ in stages]
    for _ in range(2):
        scratch += [dma((2, modes, radix - 1)) for _, radix, _, _ in stages]
    scratch += [dma((2, radix - 1)) for _, radix, _, _ in stages]
    updated, probe_direction = pl.pallas_call(
        functools.partial(kernel, tiles, stages),
        out_shape=(
            jax.ShapeDtypeStruct((2, f, columns), f32),
            jax.ShapeDtypeStruct((modes, f, 2 * f), f32),
        ),
        in_specs=[vmem, vmem, vmem, smem, smem, vmem, vmem],
        out_specs=(vmem, vmem),
        scratch_shapes=scratch,
        compiler_params=pltpu.CompilerParams(
            collective_id=0, has_side_effects=True, vmem_limit_bytes=40 * 1024 * 1024
        ),
        name="ptycho_step",
    )(object_slab.transpose(1, 0, 2), probe_modes, frames, offsets, counts, fwd, inv)
    return updated.transpose(1, 0, 2), probe_direction


def solution(mesh):
    placed = (
        P(("grp", "tile"), None, None),
        P(("grp", "mode"), None, None),
        P(("grp", "tile"), None, None),
        P(("grp", "tile"), None),
        P(("grp", "tile")),
    )
    return jax.shard_map(
        functools.partial(body, mesh.shape["tile"]),
        mesh=mesh,
        in_specs=placed,
        out_specs=(P(("grp", "tile"), None, None), P(("grp", "mode"), None, None)),
        check_vma=False,
    )
```

time: 247 us -> 50.4 us (0.20)
  local copies, waits for them, and re-layouts: 77.6 us -> 5.52 us
  starting transfers between devices: 44.6 us -> 0 us
  Pallas kernels: 0 us -> 43.2 us
  waiting for transfers between devices: 43 us -> 0 us
  blocking collectives: 23.5 us -> 0 us
  other arithmetic: 19.5 us -> 0 us
  loops' own time: 18.4 us -> 0 us
  between operations: 15.3 us -> 1.39 us
  matrix products: 3.62 us -> 0 us
    dynamic_update_slice x8 -> x0, local copies, waits for them, and re-layouts: 57.5 us -> none  [the longest x4 51.7 us: add_patch(): lax.dynamic_update_slice(grad_now, old_grad + grad_patches[slot_id], (row...]
    ppermute x3 -> x0, starting transfers between devices: 44.5 us -> none  [passed_along(): return lax.ppermute(x, axis, pairs)]
    pallas_call x0 -> x1, Pallas kernels: none -> 43.2 us  [body(): pl.pallas_call(functools.partial(kernel, tiles, stages), out_shape=(jax.S...]
    psum x3 -> x0, waiting for transfers between devices: 36.2 us -> none  [the longest x1 19.2 us: solve_slots(): gradient = lax.psum(gradient, 'mode')]
    pmax x1 -> x0, blocking collectives: 23.5 us -> none  [body(): peak = lax.pmax(jnp.max(illumination), 'tile')]
    another operation x2 -> x0, loops' own time: 18.4 us -> none  [the longest x1 18.3 us: body(): lax.fori_loop(0, slots, add_patch, (empty_grad, empty_illum))]
    add x11 -> x0, other arithmetic: 9.63 us -> none  [the longest x4 4.48 us: add_patch(): old_grad + grad_patches[slot_id]]
    gather x12 -> x0, local copies, waits for them, and re-layouts: 8.22 us -> none
  transfers between devices with their start and end apart: 6 -> 0, of which waited for: 3 -> 0; matrix products, arithmetic and copies ran while one was open for 33% -> 0% of each run, Pallas kernels for 0% -> 0%
where the time goes in v1:
time: 50.4 us; the launch traced here: 50.1 us
  Pallas kernels  43.2 us (86%)
  local copies, waits for them, and re-layouts  5.52 us (11%)
  between operations  1.39 us (3%)
    pallas_call x1, Pallas kernels, body(): pl.pallas_call(functools.partial(kernel, tiles, stages), out_shape=(jax.S...  43.2 us
    unnamed x14, local copies, waits for them, and re-layouts  5.52 us

profile of v1, /device:TPU:0, one launch (start us, length us, event | category | flops | bytes accessed | tf_op | source)
XLA Modules:
  0.0 50.1 jit_solution(13860407637833348537)
XLA Ops:
  0.6 0.0 copy-start.4
  0.6 0.0 copy-start
  1.4 0.0 copy-done.4
  1.4 0.1 copy.10.offsets
  1.5 1.0 %copy.13 = f32[128,2,256]{2,0,1:T(8,128)S(1)} copy(f32[128,2,256]{2,1,0:T(2,128)} %param.7) | data formatting | bytes 524288 | tf_op args[0]
  2.4 0.0 copy-done
  2.4 0.0 copy-start.1
  2.5 0.9 %copy-done.1 = f32[4,128,128]{2,1,0:T(8,128)S(1)} copy-done((f32[4,128,128]{2,1,0:T(8,128)S(1)}, f32[4,128,128]{2,1,0:T(8,128)}, u32[]{:S(2)}) %copy-start.1) | copy-done | bytes 262168
  3.4 0.0 copy-start.2
  3.4 0.9 %copy-done.2 = bf16[256,256]{1,0:T(8,128)(2,1)S(1)} copy-done((bf16[256,256]{1,0:T(8,128)(2,1)S(1)}, bf16[256,256]{1,0:T(8,128)(2,1)}, u32[]{:S(2)}) %copy-start.2) | copy-done | bytes 131096
  4.3 0.0 copy-start.3
  4.3 0.9 %copy-done.3 = bf16[256,256]{1,0:T(8,128)(2,1)S(1)} copy-done((bf16[256,256]{1,0:T(8,128)(2,1)S(1)}, bf16[256,256]{1,0:T(8,128)(2,1)}, u32[]{:S(2)}) %copy-start.3) | copy-done | bytes 131096
  5.2 43.2 %ptycho_step.1 = (f32[2,128,256]{2,1,0:T(8,128)S(1)}, f32[4,128,256]{2,1,0:T(8,128)S(1)}) custom-call(f32[2,128,256]{2,1,0:T(8,128)S(1)} %bitcast.4, f32[4,128,256]{2,1,0:T(8,128)S(1)} %copy-done, f32[4,128,128]{2,1,0:T(8,128)S(1)} %copy-done.1, s32[4,2]{1,0:T(4,128)S(1)} %copy.10.offsets, s32[1]{0:T(128)S(6)} %copy.15.counts, ...), custom_call_target="tpu_custom_call" | custom-call | tf_op jit(solution)/shard_map/ptycho_step/pallas_call | solution.py:497
  48.4 0.9 %copy.11 = f32[128,2,256]{2,1,0:T(2,128)} copy(f32[128,2,256]{2,0,1:T(8,128)S(1)} %bitcast.5) | data formatting | bytes 524288
  49.3 0.8 %copy.16 = f32[4,128,256]{2,1,0:T(8,128)} copy(f32[4,128,256]{2,1,0:T(8,128)S(1)} %get-tuple-element.11) | data formatting | bytes 1048576
Async XLA Ops:
  0.6 0.7 %copy-start.4 = (s32[4,2]{0,1:T(2,128)S(1)}, s32[4,2]{0,1:T(2,128)}, u32[]{:S(2)}) copy-start(s32[4,2]{0,1:T(2,128)} %param.10) | copy-start | bytes 100
  0.6 1.8 %copy-start = (f32[4,128,256]{2,1,0:T(8,128)S(1)}, f32[4,128,256]{2,1,0:T(8,128)}, u32[]{:S(2)}) copy-start(f32[4,128,256]{2,1,0:T(8,128)} %probe.1) | copy-start | bytes 1572868
  2.4 1.0 %copy-start.1 = (f32[4,128,128]{2,1,0:T(8,128)S(1)}, f32[4,128,128]{2,1,0:T(8,128)}, u32[]{:S(2)}) copy-start(f32[4,128,128]{2,1,0:T(8,128)} %frames.1) | copy-start | bytes 786436
  3.4 0.9 %copy-start.2 = (bf16[256,256]{1,0:T(8,128)(2,1)S(1)}, bf16[256,256]{1,0:T(8,128)(2,1)}, u32[]{:S(2)}) copy-start(bf16[256,256]{1,0:T(8,128)(2,1)} %constant.5.clone.inv) | copy-start | bytes 393220
  4.3 0.9 %copy-start.3 = (bf16[256,256]{1,0:T(8,128)(2,1)S(1)}, bf16[256,256]{1,0:T(8,128)(2,1)}, u32[]{:S(2)}) copy-start(bf16[256,256]{1,0:T(8,128)(2,1)} %constant.4.clone.fwd) | copy-start | bytes 393220

commit v2 on v1

--- a/solution.py
+++ b/solution.py
@@ -12,14 +12,13 @@
 MIN_ROWS = 8
 
 
-def dft_matrices():
+def dft_table():
     indices = np.arange(FRAME)
     phases = (indices[:, None] * indices[None, :] % FRAME) * (2.0 * np.pi / FRAME)
     cos_part = np.cos(phases) / np.sqrt(FRAME)
     sin_part = -np.sin(phases) / np.sqrt(FRAME)
-    fwd = np.block([[cos_part, sin_part], [-sin_part, cos_part]])
-    inv = np.block([[cos_part, -sin_part], [sin_part, cos_part]])
-    return fwd.astype(jnp.bfloat16), inv.astype(jnp.bfloat16)
+    table = np.concatenate([cos_part, sin_part], 1)
+    return table.astype(jnp.bfloat16).astype(np.float32)
 
 
 def stages_of(tiles):
@@ -45,14 +44,19 @@
     tiles,
     stages,
     obj,
+    probe_given,
+    frames_given,
+    offsets,
+    counts,
+    table_given,
+    obj_out,
+    probe_out,
     probe,
     frames,
-    offsets,
-    counts,
+    table,
     fwd,
     inv,
-    obj_out,
-    probe_out,
+    load_sem,
     ext,
     power_probe,
     ext_split,
@@ -104,10 +108,19 @@
     def pair(sem, *at):
         return (sem.at[(0, *at)], sem.at[(1, *at)])
 
-    own_power = jnp.zeros((f, f), jnp.float32)
-    for k in range(modes):
-        own_power += probe[k, :, :f] ** 2 + probe[k, :, f:] ** 2
-    power_probe[0] = own_power
+    loads = [
+        pltpu.make_async_copy(src, dst, load_sem.at[j])
+        for j, (src, dst) in enumerate(
+            [
+                (probe_given, probe),
+                (obj, ext.at[:, pl.ds(0, f)]),
+                (table_given, table),
+                (frames_given, frames),
+            ]
+        )
+    ]
+    for load in loads:
+        load.start()
 
     barrier = pltpu.get_barrier_semaphore()
 
@@ -140,9 +153,17 @@
     def _():
         halo.start()
 
+    loads[0].wait()
+    own_power = jnp.zeros((f, f), jnp.float32)
+    for k in range(modes):
+        own_power += probe[k, :, :f] ** 2 + probe[k, :, f:] ** 2
+    power_probe[0] = own_power
     pp_copy = remote(power_probe.at[0], power_probe.at[1], pair(pp_sem), mode=other)
     pp_copy.start()
-    ext[:, :f, :] = obj[...]
+
+    def each(step):
+        for s in range(slots):
+            step(s, 0)
 
     def live(s):
         return jnp.clip(counts[0] - s, 0, 1).astype(jnp.float32)
@@ -161,8 +182,8 @@
         return jnp.where(apart == by, 1.0, 0.0).astype(jnp.float32)
 
     def spread(s, values):
-        across = shifts(f, 2 * f, offsets[s, 1]).astype(jnp.bfloat16)
-        down = (shifts(2 * f, f, offsets[s, 0]) * live(s)).astype(jnp.bfloat16)
+        across = shifts(f, 2 * f, offsets[1, s]).astype(jnp.bfloat16)
+        down = (shifts(2 * f, f, offsets[0, s]) * live(s)).astype(jnp.bfloat16)
         wide = dot(jnp.concatenate(split(values), 0), across).astype(jnp.bfloat16)
         return dot(jnp.concatenate([down, down], 1), wide)
 
@@ -174,7 +195,7 @@
         illum[...] += spread(s, probe_power)
         return carry
 
-    lax.fori_loop(0, slots, light, 0)
+    each(light)
     illum_copy = remote(illum.at[pl.ds(f, f)], illum_in, pair(illum_sem), tile=right)
 
     @pl.when(has_right)
@@ -195,13 +216,14 @@
     def _():
         ext[:, f:, :] = jnp.zeros((2, f, 2 * f), jnp.float32)
 
+    loads[1].wait()
     for part in range(2):
         for j, piece in enumerate(split(ext[part])):
             ext_split[:, (2 * part + j) * 2 * f : (2 * part + j + 1) * 2 * f] = piece
 
     def window(s):
-        down = (shifts(f, 2 * f, offsets[s, 0]) * live(s)).astype(jnp.bfloat16)
-        across = shifts(2 * f, f, offsets[s, 1]).astype(jnp.bfloat16)
+        down = (shifts(f, 2 * f, offsets[0, s]) * live(s)).astype(jnp.bfloat16)
+        across = shifts(2 * f, f, offsets[1, s]).astype(jnp.bfloat16)
         rows = dot(down, ext_split[...]).astype(jnp.bfloat16)
         both = jnp.concatenate([rows[:, : 4 * f], rows[:, 4 * f :]], 0)
         return dot(both, jnp.concatenate([across, across], 0))
@@ -240,7 +262,13 @@
         power_copy(s).start()
         return carry
 
-    lax.fori_loop(0, slots, forward, 0)
+    loads[2].wait()
+    for ref, sign in ((fwd, 1.0), (inv, -1.0)):
+        ref[:f, :f] = table[:, :f].astype(jnp.bfloat16)
+        ref[f:, f:] = table[:, :f].astype(jnp.bfloat16)
+        ref[:f, f:] = (sign * table[:, f:]).astype(jnp.bfloat16)
+        ref[f:, :f] = (-sign * table[:, f:]).astype(jnp.bfloat16)
+    each(forward)
 
     @pl.when(has_left)
     def _():
@@ -286,7 +314,8 @@
         )
         return carry
 
-    lax.fori_loop(0, slots, rescale, 0)
+    loads[3].wait()
+    each(rescale)
 
     starts = [0]
     for at, radix, rows, after in stages:
@@ -384,7 +413,7 @@
                 grad[1, s] += gi
             return carry
 
-        lax.fori_loop(0, slots, backward, 0)
+        each(backward)
         if p == len(groups) - 1:
             grad_copy = remote(grad.at[other], grad_in, pair(grad_sem), mode=other)
             grad_copy.start()
@@ -406,7 +435,7 @@
         gext[...] += spread(s, grad[core, s] + grad_in[s])
         return carry
 
-    lax.fori_loop(0, slots, gather_up, 0)
+    each(gather_up)
     spill_copy = remote(gext.at[pl.ds(f, f)], spill_in, pair(spill_sem), tile=right)
 
     @pl.when(has_right)
@@ -431,7 +460,7 @@
         spill_in[...] = jnp.zeros_like(spill_in)
 
     peak = jnp.max(peaks[n_st])
-    obj_out[core] = obj[core] + (gext[:f] + spill_in[...]) / (illum[:f] + 0.1 * peak)
+    obj_out[core] = ext[core, :f] + (gext[:f] + spill_in[...]) / (illum[:f] + 0.1 * peak)
     upd_copy = remote(obj_out.at[core], obj_out.at[core], pair(upd_sem), mode=other)
     upd_copy.start()
 
@@ -458,12 +487,19 @@
     stages = stages_of(tiles)
     slots, modes = frames.shape[0], probe_modes.shape[0]
     columns = object_slab.shape[2]
-    fwd, inv = dft_matrices()
+    table = dft_table()
     f32 = jnp.float32
     vmem = pl.BlockSpec(memory_space=pltpu.VMEM)
+    hbm = pl.BlockSpec(memory_space=pltpu.HBM)
     smem = pl.BlockSpec(memory_space=pltpu.SMEM)
     dma = pltpu.SemaphoreType.DMA
     scratch = [
+        pltpu.VMEM(probe_modes.shape, f32),
+        pltpu.VMEM(frames.shape, f32),
+        pltpu.VMEM(table.shape, f32),
+        pltpu.VMEM((2 * f, 2 * f), jnp.bfloat16),
+        pltpu.VMEM((2 * f, 2 * f), jnp.bfloat16),
+        dma((4,)),
         pltpu.VMEM((2, 2 * f, columns), f32),
         pltpu.VMEM((2, f, f), f32),
         pltpu.VMEM((2 * f, 4 * columns), jnp.bfloat16),
@@ -500,14 +536,14 @@
             jax.ShapeDtypeStruct((2, f, columns), f32),
             jax.ShapeDtypeStruct((modes, f, 2 * f), f32),
         ),
-        in_specs=[vmem, vmem, vmem, smem, smem, vmem, vmem],
+        in_specs=[hbm, hbm, hbm, smem, smem, hbm],
         out_specs=(vmem, vmem),
         scratch_shapes=scratch,
         compiler_params=pltpu.CompilerParams(
-            collective_id=0, has_side_effects=True, vmem_limit_bytes=40 * 1024 * 1024
+            collective_id=0, has_side_effects=True, vmem_limit_bytes=60 * 1024 * 1024
         ),
         name="ptycho_step",
-    )(object_slab.transpose(1, 0, 2), probe_modes, frames, offsets, counts, fwd, inv)
+    )(object_slab.transpose(1, 0, 2), probe_modes, frames, offsets.T, counts, table)
     return updated.transpose(1, 0, 2), probe_direction
 
 

time: 50.4 us -> 50.5 us (level)
  Pallas kernels: 43.2 us -> 44.6 us
  local copies, waits for them, and re-layouts: 5.52 us -> 4.38 us
    pallas_call x1, Pallas kernels: 43.2 us -> 44.6 us  [body(): pl.pallas_call(functools.partial(kernel, tiles, stages), out_shape=(jax.S...]
    unnamed x14 -> x5, local copies, waits for them, and re-layouts: 5.52 us -> 4.38 us
where the time goes in v2:
time: 50.5 us; the launch traced here: 50.3 us
  Pallas kernels  44.6 us (88%)
  local copies, waits for them, and re-layouts  4.38 us (9%)
  between operations  1.29 us (3%)
    pallas_call x1, Pallas kernels, body(): pl.pallas_call(functools.partial(kernel, tiles, stages), out_shape=(jax.S...  44.6 us
    unnamed x5, local copies, waits for them, and re-layouts  4.38 us

profile of v2, /device:TPU:0, one launch (start us, length us, event | category | flops | bytes accessed | tf_op | source)
XLA Modules:
  0.0 50.3 jit_solution(2710989797005623311)
XLA Ops:
  1.3 1.7 %copy.11 = f32[128,2,256]{2,0,1:T(8,128)} copy(f32[128,2,256]{2,1,0:T(2,128)} %param.6) | data formatting | bytes 524288 | tf_op args[0]
  2.9 44.6 %ptycho_step.1 = (f32[2,128,256]{2,1,0:T(8,128)}, f32[4,128,256]{2,1,0:T(8,128)}) custom-call(f32[2,128,256]{2,1,0:T(8,128)} %bitcast.5, f32[4,128,256]{2,1,0:T(8,128)} %probe_given.1, f32[4,128,128]{2,1,0:T(8,128)} %frames_given.1, s32[2,4]{1,0:T(2,128)} %bitcast.7, s32[1]{0:T(128)S(6)} %copy.13.counts, f32[128,256]{1,0:T(8,128)} %constant.2.clone.table_given), custom_call_target="tpu_custom_call" | custom-call | tf_op jit(solution)/shard_map/ptycho_step/pallas_call | solution.py:533
  47.5 0.0 copy-start
  47.5 1.9 %copy.9 = f32[128,2,256]{2,1,0:T(2,128)} copy(f32[128,2,256]{2,0,1:T(8,128)} %bitcast.6) | data formatting | bytes 524288
  49.5 0.0 copy-done
  49.5 0.8 %copy.14 = f32[4,128,256]{2,1,0:T(8,128)} copy(f32[4,128,256]{2,1,0:T(8,128)S(1)} %copy-done) | data formatting | bytes 1048576
Async XLA Ops:
  47.5 1.9 %copy-start = (f32[4,128,256]{2,1,0:T(8,128)S(1)}, f32[4,128,256]{2,1,0:T(8,128)}, u32[]{:S(2)}) copy-start(f32[4,128,256]{2,1,0:T(8,128)} %get-tuple-element.11) | copy-start | bytes 1572868

commit v3 on v2

--- a/solution.py
+++ b/solution.py
@@ -428,6 +428,18 @@
         if i + 1 < n_st:
             peak_start(i + 1)
 
+    def advance(i, k):
+        rs_finish(i, (k,))
+        if i + 1 < n_st:
+            rs_start(i + 1, (k,))
+        else:
+            finish_sum((k,))
+            ag_start(i, (k,))
+
+    early = groups[0]
+    for k in early:
+        advance(0, k)
+
     grad_copy.wait()
     gext[...] = jnp.zeros_like(gext)
 
@@ -443,13 +455,9 @@
         spill_copy.start()
 
     for i in range(n_st):
-        for ks in groups:
-            rs_finish(i, ks)
-            if i + 1 < n_st:
-                rs_start(i + 1, ks)
-            else:
-                finish_sum(ks)
-                ag_start(i, ks)
+        for k in range(modes):
+            if i > 0 or k not in early:
+                advance(i, k)
 
     @pl.when(has_left)
     def _():
@@ -465,10 +473,10 @@
     upd_copy.start()
 
     for i in reversed(range(n_st)):
-        for ks in groups:
-            ag_finish(i, ks)
+        for k in range(modes):
+            ag_finish(i, (k,))
             if i > 0:
-                ag_start(i - 1, ks)
+                ag_start(i - 1, (k,))
 
     upd_copy.wait()
 

time: 50.5 us -> 48.5 us (0.960)
  Pallas kernels: 44.6 us -> 42.6 us
    pallas_call x1, Pallas kernels: 44.6 us -> 42.6 us  [body(): pl.pallas_call(functools.partial(kernel, tiles, stages), out_shape=(jax.S...]
where the time goes in v3:
time: 48.5 us; the launch traced here: 48.3 us
  Pallas kernels  42.6 us (88%)
  local copies, waits for them, and re-layouts  4.38 us (9%)
  between operations  1.29 us (3%)
    pallas_call x1, Pallas kernels, body(): pl.pallas_call(functools.partial(kernel, tiles, stages), out_shape=(jax.S...  42.6 us
    unnamed x5, local copies, waits for them, and re-layouts  4.38 us

profile of v3, /device:TPU:0, one launch (start us, length us, event | category | flops | bytes accessed | tf_op | source)
XLA Modules:
  0.0 48.3 jit_solution(11384864299853442047)
XLA Ops:
  1.3 1.7 %copy.11 = f32[128,2,256]{2,0,1:T(8,128)} copy(f32[128,2,256]{2,1,0:T(2,128)} %param.6) | data formatting | bytes 524288 | tf_op args[0]
  2.9 42.6 %ptycho_step.1 = (f32[2,128,256]{2,1,0:T(8,128)}, f32[4,128,256]{2,1,0:T(8,128)}) custom-call(f32[2,128,256]{2,1,0:T(8,128)} %bitcast.5, f32[4,128,256]{2,1,0:T(8,128)} %probe_given.1, f32[4,128,128]{2,1,0:T(8,128)} %frames_given.1, s32[2,4]{1,0:T(2,128)} %bitcast.7, s32[1]{0:T(128)S(6)} %copy.13.counts, f32[128,256]{1,0:T(8,128)} %constant.2.clone.table_given), custom_call_target="tpu_custom_call" | custom-call | tf_op jit(solution)/shard_map/ptycho_step/pallas_call | solution.py:541
  45.6 0.0 copy-start
  45.6 1.9 %copy.9 = f32[128,2,256]{2,1,0:T(2,128)} copy(f32[128,2,256]{2,0,1:T(8,128)} %bitcast.6) | data formatting | bytes 524288
  47.5 0.0 copy-done
  47.5 0.8 %copy.14 = f32[4,128,256]{2,1,0:T(8,128)} copy(f32[4,128,256]{2,1,0:T(8,128)S(1)} %copy-done) | data formatting | bytes 1048576
Async XLA Ops:
  45.6 1.9 %copy-start = (f32[4,128,256]{2,1,0:T(8,128)S(1)}, f32[4,128,256]{2,1,0:T(8,128)}, u32[]{:S(2)}) copy-start(f32[4,128,256]{2,1,0:T(8,128)} %get-tuple-element.11) | copy-start | bytes 1572868

commit v4 on v3

--- a/solution.py
+++ b/solution.py
@@ -58,6 +58,7 @@
     inv,
     load_sem,
     ext,
+    updated,
     power_probe,
     ext_split,
     illum,
@@ -113,7 +114,7 @@
         for j, (src, dst) in enumerate(
             [
                 (probe_given, probe),
-                (obj, ext.at[:, pl.ds(0, f)]),
+                (obj, ext.at[pl.ds(0, f)]),
                 (table_given, table),
                 (frames_given, frames),
             ]
@@ -147,7 +148,11 @@
     beside = jnp.minimum(me, 1) + jnp.minimum(tiles - 1 - me, 1)
     pl.semaphore_wait(barrier, greeted + beside)
 
-    halo = remote(obj.at[core], ext.at[core, pl.ds(f, f)], pair(halo_sem), tile=left)
+    half_rows = f // 2
+    landed = ext.at[pl.ds(f + core * half_rows, half_rows)]
+    halo = remote(
+        obj.at[pl.ds(core * half_rows, half_rows)], landed, pair(halo_sem), tile=left
+    )
 
     @pl.when(has_left)
     def _():
@@ -202,9 +207,7 @@
     def _():
         illum_copy.start()
 
-    relay = remote(
-        ext.at[core, pl.ds(f, f)], ext.at[core, pl.ds(f, f)], pair(relay_sem), mode=other
-    )
+    relay = remote(landed, landed, pair(relay_sem), mode=other)
 
     @pl.when(has_right)
     def _():
@@ -214,11 +217,11 @@
 
     @pl.when(jnp.logical_not(has_right))
     def _():
-        ext[:, f:, :] = jnp.zeros((2, f, 2 * f), jnp.float32)
+        ext[f:] = jnp.zeros((f, 2, 2 * f), jnp.float32)
 
     loads[1].wait()
     for part in range(2):
-        for j, piece in enumerate(split(ext[part])):
+        for j, piece in enumerate(split(ext[:, part, :])):
             ext_split[:, (2 * part + j) * 2 * f : (2 * part + j + 1) * 2 * f] = piece
 
     def window(s):
@@ -468,17 +471,20 @@
         spill_in[...] = jnp.zeros_like(spill_in)
 
     peak = jnp.max(peaks[n_st])
-    obj_out[core] = ext[core, :f] + (gext[:f] + spill_in[...]) / (illum[:f] + 0.1 * peak)
-    upd_copy = remote(obj_out.at[core], obj_out.at[core], pair(upd_sem), mode=other)
+    here = jnp.where(core == 0, ext[:f, 0, :], ext[:f, 1, :])
+    updated[core] = here + (gext[:f] + spill_in[...]) / (illum[:f] + 0.1 * peak)
+    upd_copy = remote(updated.at[core], updated.at[core], pair(upd_sem), mode=other)
     upd_copy.start()
 
     for i in reversed(range(n_st)):
+        if i == 0:
+            upd_copy.wait()
+            for part in range(2):
+                obj_out[:, part, :] = updated[part]
         for k in range(modes):
             ag_finish(i, (k,))
             if i > 0:
                 ag_start(i - 1, (k,))
-
-    upd_copy.wait()
 
     @pl.when(has_left)
     def _():
@@ -508,7 +514,8 @@
         pltpu.VMEM((2 * f, 2 * f), jnp.bfloat16),
         pltpu.VMEM((2 * f, 2 * f), jnp.bfloat16),
         dma((4,)),
-        pltpu.VMEM((2, 2 * f, columns), f32),
+        pltpu.VMEM((2 * f, 2, columns), f32),
+        pltpu.VMEM((2, f, columns), f32),
         pltpu.VMEM((2, f, f), f32),
         pltpu.VMEM((2 * f, 4 * columns), jnp.bfloat16),
         pltpu.VMEM((2 * f, columns), f32),
@@ -538,10 +545,10 @@
     for _ in range(2):
         scratch += [dma((2, modes, radix - 1)) for _, radix, _, _ in stages]
     scratch += [dma((2, radix - 1)) for _, radix, _, _ in stages]
-    updated, probe_direction = pl.pallas_call(
+    return pl.pallas_call(
         functools.partial(kernel, tiles, stages),
         out_shape=(
-            jax.ShapeDtypeStruct((2, f, columns), f32),
+            jax.ShapeDtypeStruct((f, 2, columns), f32),
             jax.ShapeDtypeStruct((modes, f, 2 * f), f32),
         ),
         in_specs=[hbm, hbm, hbm, smem, smem, hbm],
@@ -551,8 +558,7 @@
             collective_id=0, has_side_effects=True, vmem_limit_bytes=60 * 1024 * 1024
         ),
         name="ptycho_step",
-    )(object_slab.transpose(1, 0, 2), probe_modes, frames, offsets.T, counts, table)
-    return updated.transpose(1, 0, 2), probe_direction
+    )(object_slab, probe_modes, frames, offsets.T, counts, table)
 
 
 def solution(mesh):

time: 48.5 us -> 48.6 us (level)
  Pallas kernels: 42.6 us -> 44.6 us
  local copies, waits for them, and re-layouts: 4.38 us -> 2.52 us
    pallas_call x1, Pallas kernels: 42.6 us -> 44.6 us  [body(): pl.pallas_call(functools.partial(kernel, tiles, stages), out_shape=(jax.S...]
    unnamed x5 -> x4, local copies, waits for them, and re-layouts: 4.38 us -> 2.52 us
where the time goes in v4:
time: 48.6 us; the launch traced here: 48.5 us
  Pallas kernels  44.6 us (92%)
  local copies, waits for them, and re-layouts  2.52 us (5%)
  between operations  1.29 us (3%)
    pallas_call x1, Pallas kernels, body(): pl.pallas_call(functools.partial(kernel, tiles, stages), out_shape=(jax.S...  44.6 us
    unnamed x4, local copies, waits for them, and re-layouts  2.52 us

profile of v4, /device:TPU:0, one launch (start us, length us, event | category | flops | bytes accessed | tf_op | source)
XLA Modules:
  0.0 48.5 jit_solution(7430563650047976240)
XLA Ops:
  1.3 44.6 %ptycho_step.1 = (f32[128,2,256]{2,1,0:T(2,128)}, f32[4,128,256]{2,1,0:T(8,128)}) custom-call(f32[128,2,256]{2,1,0:T(2,128)} %obj.1, f32[4,128,256]{2,1,0:T(8,128)} %probe_given.1, f32[4,128,128]{2,1,0:T(8,128)} %frames_given.1, s32[2,4]{1,0:T(2,128)} %bitcast.1, s32[1]{0:T(128)S(6)} %copy.10.counts, f32[128,256]{1,0:T(8,128)} %constant.2.clone.table_given), custom_call_target="tpu_custom_call" | custom-call | tf_op jit(solution)/shard_map/ptycho_step/pallas_call | solution.py:548
  45.9 0.0 copy-start
  45.9 1.7 %copy.11 = f32[128,2,256]{2,1,0:T(2,128)} copy(f32[128,2,256]{2,1,0:T(2,128)} %get-tuple-element.4) | data formatting | bytes 524288
  47.7 0.0 copy-done
  47.7 0.8 %copy.12 = f32[4,128,256]{2,1,0:T(8,128)} copy(f32[4,128,256]{2,1,0:T(8,128)S(1)} %copy-done) | data formatting | bytes 1048576
Async XLA Ops:
  45.9 1.7 %copy-start = (f32[4,128,256]{2,1,0:T(8,128)S(1)}, f32[4,128,256]{2,1,0:T(8,128)}, u32[]{:S(2)}) copy-start(f32[4,128,256]{2,1,0:T(8,128)} %get-tuple-element.5) | copy-start | bytes 1572868

commit v5 on v3

--- a/solution.py
+++ b/solution.py
@@ -26,11 +26,11 @@
     assert tiles == 1 << bits
     stages, at, rows = [], 0, FRAME
     while at < bits:
-        radix = 2 if at == 0 or bits - at == 1 else 4
+        radix = 2
         after = rows // radix if rows // radix >= MIN_ROWS else rows
         stages.append((at, radix, rows, after))
         rows = after
-        at += 1 if radix == 2 else 2
+        at += 1
     return stages
 
 

time: 48.5 us -> 52.3 us (1.078)
  Pallas kernels: 42.6 us -> 46.4 us
    pallas_call x1, Pallas kernels: 42.6 us -> 46.4 us  [body(): pl.pallas_call(functools.partial(kernel, tiles, stages), out_shape=(jax.S...]
where the time goes in v5:
time: 52.3 us; the launch traced here: 52.1 us
  Pallas kernels  46.4 us (89%)
  local copies, waits for them, and re-layouts  4.38 us (8%)
  between operations  1.29 us (2%)
    pallas_call x1, Pallas kernels, body(): pl.pallas_call(functools.partial(kernel, tiles, stages), out_shape=(jax.S...  46.4 us
    unnamed x5, local copies, waits for them, and re-layouts  4.38 us

profile of v5, /device:TPU:0, one launch (start us, length us, event | category | flops | bytes accessed | tf_op | source)
XLA Modules:
  0.0 52.1 jit_solution(6171834113939243963)
XLA Ops:
  1.3 1.7 %copy.11 = f32[128,2,256]{2,0,1:T(8,128)} copy(f32[128,2,256]{2,1,0:T(2,128)} %param.6) | data formatting | bytes 524288 | tf_op args[0]
  2.9 46.4 %ptycho_step.1 = (f32[2,128,256]{2,1,0:T(8,128)}, f32[4,128,256]{2,1,0:T(8,128)}) custom-call(f32[2,128,256]{2,1,0:T(8,128)} %bitcast.5, f32[4,128,256]{2,1,0:T(8,128)} %probe_given.1, f32[4,128,128]{2,1,0:T(8,128)} %frames_given.1, s32[2,4]{1,0:T(2,128)} %bitcast.7, s32[1]{0:T(128)S(6)} %copy.13.counts, f32[128,256]{1,0:T(8,128)} %constant.2.clone.table_given), custom_call_target="tpu_custom_call" | custom-call | tf_op jit(solution)/shard_map/ptycho_step/pallas_call | solution.py:541
  49.4 0.0 copy-start
  49.4 1.9 %copy.9 = f32[128,2,256]{2,1,0:T(2,128)} copy(f32[128,2,256]{2,0,1:T(8,128)} %bitcast.6) | data formatting | bytes 524288
  51.3 0.0 copy-done
  51.3 0.8 %copy.14 = f32[4,128,256]{2,1,0:T(8,128)} copy(f32[4,128,256]{2,1,0:T(8,128)S(1)} %copy-done) | data formatting | bytes 1048576
Async XLA Ops:
  49.4 1.9 %copy-start = (f32[4,128,256]{2,1,0:T(8,128)S(1)}, f32[4,128,256]{2,1,0:T(8,128)}, u32[]{:S(2)}) copy-start(f32[4,128,256]{2,1,0:T(8,128)} %get-tuple-element.11) | copy-start | bytes 1572868

commit v6 on v3

--- a/solution.py
+++ b/solution.py
@@ -162,8 +162,7 @@
     pp_copy.start()
 
     def each(step):
-        for s in range(slots):
-            step(s, 0)
+        lax.fori_loop(0, slots, step, 0)
 
     def live(s):
         return jnp.clip(counts[0] - s, 0, 1).astype(jnp.float32)

time: 48.5 us -> 49 us (1.010)
  Pallas kernels: 42.6 us -> 43.1 us
    pallas_call x1, Pallas kernels: 42.6 us -> 43.1 us  [body(): pl.pallas_call(functools.partial(kernel, tiles, stages), out_shape=(jax.S...]
where the time goes in v6:
time: 49 us; the launch traced here: 48.8 us
  Pallas kernels  43.1 us (88%)
  local copies, waits for them, and re-layouts  4.38 us (9%)
  between operations  1.29 us (3%)
    pallas_call x1, Pallas kernels, body(): pl.pallas_call(functools.partial(kernel, tiles, stages), out_shape=(jax.S...  43.1 us
    unnamed x5, local copies, waits for them, and re-layouts  4.38 us

profile of v6, /device:TPU:0, one launch (start us, length us, event | category | flops | bytes accessed | tf_op | source)
XLA Modules:
  0.0 48.8 jit_solution(10471102364157424183)
XLA Ops:
  1.3 1.7 %copy.11 = f32[128,2,256]{2,0,1:T(8,128)} copy(f32[128,2,256]{2,1,0:T(2,128)} %param.6) | data formatting | bytes 524288 | tf_op args[0]
  2.9 43.1 %ptycho_step.1 = (f32[2,128,256]{2,1,0:T(8,128)}, f32[4,128,256]{2,1,0:T(8,128)}) custom-call(f32[2,128,256]{2,1,0:T(8,128)} %bitcast.5, f32[4,128,256]{2,1,0:T(8,128)} %probe_given.1, f32[4,128,128]{2,1,0:T(8,128)} %frames_given.1, s32[2,4]{1,0:T(2,128)} %bitcast.7, s32[1]{0:T(128)S(6)} %copy.13.counts, f32[128,256]{1,0:T(8,128)} %constant.2.clone.table_given), custom_call_target="tpu_custom_call" | custom-call | tf_op jit(solution)/shard_map/ptycho_step/pallas_call | solution.py:540
  46.1 0.0 copy-start
  46.1 1.9 %copy.9 = f32[128,2,256]{2,1,0:T(2,128)} copy(f32[128,2,256]{2,0,1:T(8,128)} %bitcast.6) | data formatting | bytes 524288
  48.0 0.0 copy-done
  48.0 0.8 %copy.14 = f32[4,128,256]{2,1,0:T(8,128)} copy(f32[4,128,256]{2,1,0:T(8,128)S(1)} %copy-done) | data formatting | bytes 1048576
Async XLA Ops:
  46.1 1.9 %copy-start = (f32[4,128,256]{2,1,0:T(8,128)S(1)}, f32[4,128,256]{2,1,0:T(8,128)}, u32[]{:S(2)}) copy-start(f32[4,128,256]{2,1,0:T(8,128)} %get-tuple-element.11) | copy-start | bytes 1572868
